TPU v7x, 256 devices: a whole 4x4x8 slice. The times are simulated.
256 devices in a mesh: blk: 64 (over x, z, core), smp: 4 (over y).
Axes of the slice: x: 4, y: 4, z: 8, core: 2. Of those that a mesh axis runs over, the one named last changes fastest.
Arguments:
- encodings: bfloat16 [1024, 57344], P('smp', 'blk'), may hold values from -1 to 1
- hidden_pre: bfloat16 [1024, 8192], P('smp', 'blk'), may hold values from -6 to 6
- cotangent: bfloat16 [1024, 688128], P('smp', 'blk'), may hold values from -0.75 to 0.75
- out_weights: bfloat16 [10752, 128, 128], P('blk'), may hold values from -0.0390625 to 0.0390625
- out_contacts: int32 [5376, 2], P('blk'), may hold values from 0 to 63, all different within a row
- in_contacts: int32 [448, 4], P('blk'), may hold values from 0 to 63, all different within a row
Outputs:
- out_weight_grad: bfloat16 [10752, 128, 128], P(('blk', 'smp'))
- in_weight_grad: bfloat16 [1792, 128, 128], P(('blk', 'smp'))
Inputs may be any that keep to these rules, and one draw needn't show every extreme that they name: `out_contacts`: each row names 2 different hidden blocks, and every hidden block is named by some row. `in_contacts`: each row names 4 different hidden blocks, and every hidden block is named by some row.
All inputs are finite; a program needn't handle non-finite values.
Results may differ from a plain program's by a relative error of at most 0.0051.
Values may be sent and summed in bfloat16 or wider, within the bound.
No kernel may reach another device: no remote copies, remote signals or barrier semaphores. Data moves between devices by JAX's collectives and lax.ppermute only.
A program may use at most 128 MiB of HBM per device.

v0:
```python
import jax
import jax.numpy as jnp
from jax import lax
from jax.sharding import PartitionSpec as P


def silu_slope(values):
    sigma = jax.nn.sigmoid(values)
    return sigma * (1.0 + values * (1.0 - sigma))


def per_device(encodings, hidden_pre, cotangent, out_weights, out_contacts, in_contacts):
    sample_rows = cotangent.shape[0]
    block_size = out_weights.shape[1]
    out_local, per_out = out_contacts.shape
    in_local, per_in = in_contacts.shape
    pre_whole = lax.all_gather(hidden_pre, "blk", axis=1, tiled=True)
    hid_count = pre_whole.shape[1] // block_size
    pre_blocks = pre_whole.reshape(sample_rows, hid_count, block_size)
    activation = jax.nn.silu(pre_blocks.astype(jnp.float32)).astype(jnp.bfloat16)
    out_index = out_contacts.reshape(-1)
    in_index = in_contacts.reshape(-1)
    activ_taken = jnp.take(activation, out_index, axis=1).reshape(
        sample_rows, out_local, per_out, block_size
    )
    cot_blocks = cotangent.reshape(sample_rows, out_local, block_size)
    out_terms = jnp.einsum(
        "sokb,soc->okbc", activ_taken, cot_blocks, preferred_element_type=jnp.float32
    )
    out_terms = out_terms.reshape(out_local * per_out, block_size, block_size)
    out_grad = lax.psum_scatter(out_terms, "smp", scatter_dimension=0, tiled=True).astype(
        jnp.bfloat16
    )
    weight_view = out_weights.reshape(out_local, per_out, block_size, block_size)
    partial_terms = jnp.einsum(
        "soc,okbc->oksb", cot_blocks, weight_view, preferred_element_type=jnp.float32
    )
    partial_terms = partial_terms.reshape(out_local * per_out, sample_rows, block_size)
    hidden_terms = jax.ops.segment_sum(partial_terms, out_index, num_segments=hid_count)
    summed = lax.psum(hidden_terms, "blk")
    summed_taken = jnp.swapaxes(jnp.take(summed, in_index, axis=0), 0, 1)
    pre_taken = jnp.take(pre_blocks, in_index, axis=1).astype(jnp.float32)
    grad_taken = (summed_taken * silu_slope(pre_taken)).astype(jnp.bfloat16)
    grad_view = grad_taken.reshape(sample_rows, in_local, per_in, block_size)
    enc_blocks = encodings.reshape(sample_rows, in_local, block_size)
    in_terms = jnp.einsum(
        "sib,sikc->ikbc", enc_blocks, grad_view, preferred_element_type=jnp.float32
    )
    in_terms = in_terms.reshape(in_local * per_in, block_size, block_size)
    in_grad = lax.psum_scatter(in_terms, "smp", scatter_dimension=0, tiled=True).astype(
        jnp.bfloat16
    )
    return (out_grad, in_grad)


def solution(mesh):
    in_specs = (
        P("smp", "blk"),
        P("smp", "blk"),
        P("smp", "blk"),
        P("blk", None, None),
        P("blk", None),
        P("blk", None),
    )
    out_specs = (P(("blk", "smp"), None, None), P(("blk", "smp"), None, None))
    return jax.shard_map(
        per_device, mesh=mesh, in_specs=in_specs, out_specs=out_specs, check_vma=False
    )
```

profile of v0, /device:TPU:1, one launch (start us, length us, event | category | flops | bytes accessed | tf_op | source)
XLA Modules:
  0.0 569.7 jit_solution(5942079644765487091)
XLA Ops:
  7.2 0.0 all-reduce.2.cloned.1.call-start
  7.2 8.3 %copy.36 = bf16[256,10752]{0,1:T(8,128)(2,1)} copy(bf16[256,10752]{1,0:T(8,128)(2,1)} %param.8) | data formatting | bytes 11010048 | tf_op args[2]
  15.5 14.6 %fusion.17 = f32[84,2,128,256]{3,2,1,0:T(8,128)} fusion(bf16[84,2,128,128]{3,2,1,0:T(8,128)(2,1)} %bitcast.57, bf16[256,84,128,1]{0,2,3,1:T(8,128)(2,1)} %bitcast.55), kind=kOutput, calls=%fused_computation.33 | convolution fusion | flops 1409286144 | bytes 33030144 | tf_op jit(solution)/shard_map/soc,okbc->oksb/dot_general | solution.py:35
  30.1 0.0 copy-start.3
  30.1 21.6 %copy.41 = f32[168,256,128]{2,1,0:T(8,128)} copy(f32[168,256,128]{1,2,0:T(8,128)} %bitcast.53) | data formatting | bytes 44040192 | tf_op jit(solution)/shard_map/reshape | solution.py:38
  51.7 0.0 copy-done.3
  51.7 0.1 copy.34
  51.8 0.1 reshape.144
  52.0 4.4 broadcast_in_dim.36
  56.3 51.9 %scatter_fusion = f32[64,256,128]{2,1,0:T(8,128)} fusion(f32[64,256,128]{2,1,0:T(8,128)} %broadcast_in_dim.36, s32[168]{0:T(256)S(1)} %reshape.144, f32[168,256,128]{2,1,0:T(8,128)} %copy.41), kind=kCustom, calls=%fused_computation.3 | custom fusion | flops 5505024 | bytes 66060960 | tf_op jit(solution)/shard_map/scatter-add | solution.py:39
  108.2 0.0 copy-start.1
  108.2 0.0 copy-start.2
  108.2 0.0 copy-start
  108.2 0.0 all-reduce.2.cloned.1.call-update
  108.2 0.0 all-gather.2.cloned.1.call-start
  108.3 0.8 copy-done.1
  109.0 0.7 copy.32
  109.8 0.0 all-gather.2.cloned.1.call-update
  109.8 0.0 reduce-scatter.5.cloned.1.call-start
  109.9 0.0 copy-done.2
  109.9 0.1 copy.38
  110.0 0.1 reshape.114
  110.0 0.1 reshape.111
  110.1 0.0 copy-done
  110.1 0.2 copy.44
  110.4 205.8 %all-reduce.2.cloned.1.call-done = f32[64,256,128]{2,1,0:T(8,128)} async-done(((f32[64,256,128]{2,1,0:T(8,128)}), f32[64,256,128]{2,1,0:T(8,128)}) %all-reduce.2.cloned.1.call-update) | async-done | bytes 8388624 | tf_op jit(solution)/shard_map/psum | solution.py:40
  316.2 5.9 %gather_fusion.1 = f32[28,256,128]{2,1,0:T(8,128)} fusion(f32[64,256,128]{2,1,0:T(8,128)} %all-reduce.2.cloned.1.call-done, s32[1024]{0:T(1024)S(1)} %pad_clamp_fusion), kind=kCustom, calls=%fused_computation.1 | custom fusion | bytes 7340144 | tf_op jit(solution)/shard_map/jit(_take)/gather | solution.py:41
  322.2 77.4 %all-gather.2.cloned.1.call-done = bf16[256,8192]{0,1:T(8,128)(2,1)} async-done(((bf16[256,128]{0,1:T(8,128)(2,1)}), bf16[256,8192]{0,1:T(8,128)(2,1)}) %all-gather.2.cloned.1.call-update) | async-done | bytes 4194320 | tf_op jit(solution)/shard_map/all_gather | solution.py:17
  399.6 6.4 %copy.33 = bf16[256,64,128]{2,0,1:T(8,128)(2,1)} copy(bf16[256,64,128]{0,2,1:T(8,128)(2,1)} %bitcast.61) | data formatting | bytes 8388608 | tf_op jit(solution)/shard_map/reshape | solution.py:19
  405.9 3.1 gather_fusion.2
  409.0 3.8 fusion.14
  412.8 0.8 fusion.18
  413.6 1.7 copy.47
  415.3 0.0 reduce-scatter.5.cloned.1.call-update
  415.3 0.2 reduce-scatter.3.cloned.1.call-start
  415.5 0.1 reshape.108
  415.7 0.1 copy.31
  415.8 5.1 fusion.6
  420.9 10.0 %gather_fusion = bf16[168,256,128]{2,1,0:T(8,128)(2,1)} fusion(bf16[256,64,128]{2,0,1:T(8,128)(2,1)} %fusion.6, s32[1024]{0:T(1024)S(1)} %pad_clamp_fusion.1), kind=kCustom, calls=%fused_computation | custom fusion | bytes 22020768 | tf_op jit(solution)/shard_map/jit(_take)/gather | solution.py:23
  430.9 14.7 %copy.35 = bf16[256,84,2,128]{0,3,2,1:T(8,128)(2,1)} copy(bf16[256,84,2,128]{3,0,2,1:T(8,128)(2,1)} %bitcast.54) | data formatting | bytes 22020096 | tf_op jit(solution)/shard_map/jit(_take)/gather | solution.py:23
  445.6 13.0 %fusion = f32[84,2,128,128]{3,2,1,0:T(8,128)} fusion(bf16[256,84,128,1]{0,2,3,1:T(8,128)(2,1)} %bitcast.56, bf16[256,84,2,128]{0,3,2,1:T(8,128)(2,1)} %copy.35, pred[84,2]{1,0:T(8,128)(4,1)S(1)} %copy.31), kind=kOutput, calls=%fused_computation.4 | convolution fusion | flops 1414791168 | bytes 27525288 | tf_op jit(solution)/shard_map/sokb,soc->okbc/dot_general | solution.py:27
  458.6 0.0 reduce-scatter.3.cloned.1.call-update
  458.6 0.0 reduce-scatter.5.cloned.1.call-done
  458.7 1.7 convert_element_type.23
  460.4 99.7 %reduce-scatter.3.cloned.1.call-done = f32[42,128,128]{2,1,0:T(8,128)} async-done(((f32[168,128,128]{2,1,0:T(8,128)}), f32[42,128,128]{2,1,0:T(8,128)}) %reduce-scatter.3.cloned.1.call-update) | async-done | bytes 2752528 | tf_op jit(solution)/shard_map/reduce_scatter | solution.py:31
  560.1 3.1 convert_element_type.20
  (6 shorter events, 0.0 us)
Async XLA Ops:
  7.2 309.0 %all-reduce.2.cloned.1.call-start = ((), (), s32[]{:S(2)}) async-start(), calls=%async_computation.4 | async-start | bytes 16777216 | tf_op jit(solution)/shard_map/psum | solution.py:40
  30.1 21.7 %copy-start.3 = (s32[84,2]{0,1:T(2,128)S(1)}, s32[84,2]{0,1:T(2,128)}, u32[]{:S(2)}) copy-start(s32[84,2]{0,1:T(2,128)} %param.10) | copy-start | bytes 2020
  108.2 0.8 copy-start.1
  108.2 1.7 copy-start.2
  108.2 1.9 copy-start
  108.2 291.3 %all-gather.2.cloned.1.call-start = ((), (), s32[]{:S(2)}) async-start(), calls=%async_computation.2 | async-start | bytes 4259840 | tf_op jit(solution)/shard_map/all_gather | solution.py:17
  109.8 348.9 %reduce-scatter.5.cloned.1.call-start = ((), (), s32[]{:S(2)}) async-start(), calls=%async_computation.5 | async-start | bytes 2293760 | tf_op jit(solution)/shard_map/reduce_scatter | solution.py:50
  415.3 144.8 %reduce-scatter.3.cloned.1.call-start = ((), (), s32[]{:S(2)}) async-start(), calls=%async_computation.3 | async-start | bytes 13762560 | tf_op jit(solution)/shard_map/reduce_scatter | solution.py:31
Sparse Core Ops, SparseCore 0:
  108.3 207.8 all-reduce.1
  319.9 79.5 all-gather.1
  415.4 27.0 reduce-scatter.4
  458.8 101.2 reduce-scatter.2
where the time goes:
time: 571 us; the launch traced here: 570 us
  waiting for transfers between devices  383 us (67%)
  local copies, waits for them, and re-layouts  78.6 us (14%)
  other arithmetic  65.6 us (11%)
  matrix products  28.4 us (5%)
  between operations  13.9 us (2%)
    psum x1, waiting for transfers between devices, per_device(): summed = lax.psum(hidden_terms, 'blk')  206 us
    reduce_scatter x1, waiting for transfers between devices, per_device(): lax.psum_scatter(out_terms, 'smp', scatter_dimension=0, tiled=True)  99.7 us
    all_gather x1, waiting for transfers between devices, per_device(): pre_whole = lax.all_gather(hidden_pre, 'blk', axis=1, tiled=True)  77.4 us
    scatter-add x1, other arithmetic, per_device(): jax.ops.segment_sum(partial_terms, out_index, num_segments=hid_count)  51.9 us
    gather x2, local copies, waits for them, and re-layouts, per_device(): jnp.take(activation, out_index, axis=1)  24.7 us
    reshape x1, local copies, waits for them, and re-layouts, per_device(): partial_terms.reshape(out_local * per_out, sample_rows, block_size)  21.6 us
    dot_general x1, matrix products, per_device(): jnp.einsum('soc,okbc->oksb', cot_blocks, weight_view, preferred_element_t...  14.6 us
    dot_general x1, matrix products, per_device(): jnp.einsum('sokb,soc->okbc', activ_taken, cot_blocks, preferred_element_t...  13 us
  transfers between devices with their start and end apart: 4, of which 3 were waited for; matrix products, arithmetic and copies ran while one was open for 9% of the time, Pallas kernels for 0%

commit v1 on v0

--- a/solution.py
+++ b/solution.py
@@ -14,7 +14,11 @@
     block_size = out_weights.shape[1]
     out_local, per_out = out_contacts.shape
     in_local, per_in = in_contacts.shape
-    pre_whole = lax.all_gather(hidden_pre, "blk", axis=1, tiled=True)
+    count = lax.axis_size("blk")
+    repeats = [count if d == 1 else 1 for d in range(hidden_pre.ndim)]
+    pre_whole = lax.all_to_all(
+        jnp.tile(hidden_pre, repeats), "blk", split_axis=1, concat_axis=1, tiled=True
+    )
     hid_count = pre_whole.shape[1] // block_size
     pre_blocks = pre_whole.reshape(sample_rows, hid_count, block_size)
     activation = jax.nn.silu(pre_blocks.astype(jnp.float32)).astype(jnp.bfloat16)

time: 571 us -> 505 us (0.88)
  waiting for transfers between devices: 383 us -> 307 us
  starting transfers between devices: 0.34 us -> 13.5 us
    all_gather x1 -> x0, waiting for transfers between devices: 77.4 us -> none  [per_device(): pre_whole = lax.all_gather(hidden_pre, 'blk', axis=1, tiled=True)]
    all_to_all x0 -> x1, starting transfers between devices: none -> 13.2 us  [per_device(): lax.all_to_all(jnp.tile(hidden_pre, repeats), 'blk', split_axis=1, concat...]
    reshape x1 -> x0, local copies, waits for them, and re-layouts: 6.37 us -> none  [per_device(): pre_blocks = pre_whole.reshape(sample_rows, hid_count, block_size)]
  transfers between devices with their start and end apart: 4 -> 4, of which waited for: 3 -> 2; matrix products, arithmetic and copies ran while one was open for 9% -> 30% of each run, Pallas kernels for 0% -> 0%
where the time goes in v1:
time: 505 us; the launch traced here: 503 us
  waiting for transfers between devices  307 us (61%)
  local copies, waits for them, and re-layouts  75.3 us (15%)
  other arithmetic  65.4 us (13%)
  matrix products  28.4 us (6%)
  between operations  13.8 us (3%)
  starting transfers between devices  13.5 us (3%)
    psum x1, waiting for transfers between devices, per_device(): summed = lax.psum(hidden_terms, 'blk')  204 us
    reduce_scatter x1, waiting for transfers between devices, per_device(): lax.psum_scatter(out_terms, 'smp', scatter_dimension=0, tiled=True)  103 us
    scatter-add x1, other arithmetic, per_device(): jax.ops.segment_sum(partial_terms, out_index, num_segments=hid_count)  51.7 us
    gather x2, local copies, waits for them, and re-layouts, per_device(): jnp.take(activation, out_index, axis=1)  24.7 us
    reshape x1, local copies, waits for them, and re-layouts, per_device(): partial_terms.reshape(out_local * per_out, sample_rows, block_size)  21.7 us
    dot_general x1, matrix products, per_device(): jnp.einsum('soc,okbc->oksb', cot_blocks, weight_view, preferred_element_t...  14.6 us
    all_to_all x1, starting transfers between devices, per_device(): lax.all_to_all(jnp.tile(hidden_pre, repeats), 'blk', split_axis=1, concat...  13.2 us
    dot_general x1, matrix products, per_device(): jnp.einsum('sokb,soc->okbc', activ_taken, cot_blocks, preferred_element_t...  13 us
  transfers between devices with their start and end apart: 4, of which 2 were waited for; matrix products, arithmetic and copies ran while one was open for 30% of the time, Pallas kernels for 0%

profile of v1, /device:TPU:1, one launch (start us, length us, event | category | flops | bytes accessed | tf_op | source)
XLA Modules:
  0.0 503.3 jit_solution(11449421905022996017)
XLA Ops:
  7.2 3.8 tile.2
  11.0 13.2 %all-to-all-start = ((bf16[256,64,128]{2,0,1:T(8,128)(2,1)}), bf16[256,64,128]{2,0,1:T(8,128)(2,1)}, u32[]{:S(2)}, u32[]{:S(2)}) async-start(bf16[256,64,128]{2,0,1:T(8,128)(2,1)} %tile.2), calls=%async_computation | async-start | bytes 8388608 | tf_op jit(solution)/shard_map/all_to_all | solution.py:19
  24.1 0.0 all-reduce.2.cloned.1.call-start
  24.2 8.3 %copy.18 = bf16[256,10752]{0,1:T(8,128)(2,1)} copy(bf16[256,10752]{1,0:T(8,128)(2,1)} %param.8) | data formatting | bytes 11010048 | tf_op args[2]
  32.5 14.6 %fusion.17 = f32[84,2,128,256]{3,2,1,0:T(8,128)} fusion(bf16[84,2,128,128]{3,2,1,0:T(8,128)(2,1)} %bitcast.56, bf16[256,84,128,1]{0,2,3,1:T(8,128)(2,1)} %bitcast.54), kind=kOutput, calls=%fused_computation.33 | convolution fusion | flops 1409286144 | bytes 33030144 | tf_op jit(solution)/shard_map/soc,okbc->oksb/dot_general | solution.py:39
  47.1 0.0 copy-start.2
  47.1 21.7 %copy.23 = f32[168,256,128]{2,1,0:T(8,128)} copy(f32[168,256,128]{1,2,0:T(8,128)} %bitcast.52) | data formatting | bytes 44040192 | tf_op jit(solution)/shard_map/reshape | solution.py:42
  68.7 0.0 copy-done.2
  68.7 0.1 copy.16
  68.9 0.1 reshape.149
  69.0 4.4 broadcast_in_dim.36
  73.3 51.7 %scatter_fusion = f32[64,256,128]{2,1,0:T(8,128)} fusion(f32[64,256,128]{2,1,0:T(8,128)} %broadcast_in_dim.36, s32[168]{0:T(256)S(1)} %reshape.149, f32[168,256,128]{2,1,0:T(8,128)} %copy.23), kind=kCustom, calls=%fused_computation.3 | custom fusion | flops 5505024 | bytes 66060960 | tf_op jit(solution)/shard_map/scatter-add | solution.py:43
  125.1 0.0 copy-start.1
  125.1 0.0 copy-start
  125.1 0.0 all-reduce.2.cloned.1.call-update
  125.1 0.0 reduce-scatter.5.cloned.1.call-start
  125.1 0.6 copy-done.1
  125.7 0.1 copy.20
  125.8 0.1 reshape.119
  125.9 0.1 reshape.116
  126.0 0.1 copy-done
  126.1 0.2 copy.25
  126.4 203.9 %all-reduce.2.cloned.1.call-done = f32[64,256,128]{2,1,0:T(8,128)} async-done(((f32[64,256,128]{2,1,0:T(8,128)}), f32[64,256,128]{2,1,0:T(8,128)}) %all-reduce.2.cloned.1.call-update) | async-done | bytes 8388624 | tf_op jit(solution)/shard_map/psum | solution.py:44
  330.3 6.0 %gather_fusion.1 = f32[28,256,128]{2,1,0:T(8,128)} fusion(f32[64,256,128]{2,1,0:T(8,128)} %all-reduce.2.cloned.1.call-done, s32[1024]{0:T(1024)S(1)} %pad_clamp_fusion), kind=kCustom, calls=%fused_computation.1 | custom fusion | bytes 7340144 | tf_op jit(solution)/shard_map/jit(_take)/gather | solution.py:45
  336.3 0.0 all-to-all-done
  336.3 3.1 gather_fusion.2
  339.4 3.8 fusion.14
  343.2 0.8 fusion.18
  343.9 1.7 copy.28
  345.7 0.0 reduce-scatter.5.cloned.1.call-update
  345.7 0.2 reduce-scatter.3.cloned.1.call-start
  345.9 0.1 reshape.113
  346.1 0.1 copy.15
  346.2 5.1 %fusion.6 = bf16[256,64,128]{2,0,1:T(8,128)(2,1)} fusion(bf16[256,64,128]{2,0,1:T(8,128)(2,1)} %all-to-all-done), kind=kLoop, calls=%fused_computation.12 | loop fusion | flops 12582912 | bytes 8388608 | tf_op jit(solution)/shard_map/convert_element_type | solution.py:24
  351.3 10.0 %gather_fusion = bf16[168,256,128]{2,1,0:T(8,128)(2,1)} fusion(bf16[256,64,128]{2,0,1:T(8,128)(2,1)} %fusion.6, s32[1024]{0:T(1024)S(1)} %pad_clamp_fusion.1), kind=kCustom, calls=%fused_computation | custom fusion | bytes 22020768 | tf_op jit(solution)/shard_map/jit(_take)/gather | solution.py:27
  361.3 14.7 %copy.17 = bf16[256,84,2,128]{0,3,2,1:T(8,128)(2,1)} copy(bf16[256,84,2,128]{3,0,2,1:T(8,128)(2,1)} %bitcast.53) | data formatting | bytes 22020096 | tf_op jit(solution)/shard_map/jit(_take)/gather | solution.py:27
  376.0 13.0 %fusion = f32[84,2,128,128]{3,2,1,0:T(8,128)} fusion(bf16[256,84,128,1]{0,2,3,1:T(8,128)(2,1)} %bitcast.55, bf16[256,84,2,128]{0,3,2,1:T(8,128)(2,1)} %copy.17, pred[84,2]{1,0:T(8,128)(4,1)S(1)} %copy.15), kind=kOutput, calls=%fused_computation.4 | convolution fusion | flops 1414791168 | bytes 27525288 | tf_op jit(solution)/shard_map/sokb,soc->okbc/dot_general | solution.py:31
  389.0 0.0 reduce-scatter.3.cloned.1.call-update
  389.0 0.0 reduce-scatter.5.cloned.1.call-done
  389.0 1.7 convert_element_type.23
  390.8 102.9 %reduce-scatter.3.cloned.1.call-done = f32[42,128,128]{2,1,0:T(8,128)} async-done(((f32[168,128,128]{2,1,0:T(8,128)}), f32[42,128,128]{2,1,0:T(8,128)}) %reduce-scatter.3.cloned.1.call-update) | async-done | bytes 2752528 | tf_op jit(solution)/shard_map/reduce_scatter | solution.py:35
  493.7 3.1 convert_element_type.20
  (6 shorter events, 0.0 us)
Async XLA Ops:
  11.0 325.3 %all-to-all-start = ((bf16[256,64,128]{2,0,1:T(8,128)(2,1)}), bf16[256,64,128]{2,0,1:T(8,128)(2,1)}, u32[]{:S(2)}, u32[]{:S(2)}) async-start(bf16[256,64,128]{2,0,1:T(8,128)(2,1)} %tile.2), calls=%async_computation | async-start | bytes 8388608 | tf_op jit(solution)/shard_map/all_to_all | solution.py:19
  24.1 306.1 %all-reduce.2.cloned.1.call-start = ((), (), s32[]{:S(2)}) async-start(), calls=%async_computation.4 | async-start | bytes 16777216 | tf_op jit(solution)/shard_map/psum | solution.py:44
  47.1 21.7 %copy-start.2 = (s32[84,2]{0,1:T(2,128)S(1)}, s32[84,2]{0,1:T(2,128)}, u32[]{:S(2)}) copy-start(s32[84,2]{0,1:T(2,128)} %param.10) | copy-start | bytes 2020
  125.1 0.7 copy-start.1
  125.1 1.0 copy-start
  125.1 263.9 %reduce-scatter.5.cloned.1.call-start = ((), (), s32[]{:S(2)}) async-start(), calls=%async_computation.5 | async-start | bytes 2293760 | tf_op jit(solution)/shard_map/reduce_scatter | solution.py:54
  345.7 148.0 %reduce-scatter.3.cloned.1.call-start = ((), (), s32[]{:S(2)}) async-start(), calls=%async_computation.3 | async-start | bytes 13762560 | tf_op jit(solution)/shard_map/reduce_scatter | solution.py:35
Sparse Core Ops, SparseCore 0:
  125.2 205.0 all-reduce.1
  345.8 30.3 reduce-scatter.4
  389.1 104.5 reduce-scatter.2
